TPU v7x, 32 devices: a whole 2x2x4 slice. The times are simulated.
32 devices in a mesh: seq: 16 (over z, y, core), dp: 2 (over x).
Axes of the slice: x: 2, y: 2, z: 4, core: 2. Of those that a mesh axis runs over, the one named last changes fastest.
Arguments:
- features: float32 [2, 4096, 512], P('dp', 'seq'), may hold values from -64 to 64
- norm_gain: float32 [2, 512], replicated, may hold values from 0.25 to 1.75
- filters: float32 [4, 512], replicated, may hold values from -1 to 1
- level_weights: float32 [13, 512], replicated, may hold values from -1.2 to 1.2
- glu_weight: float32 [512, 1024], P('dp'), may hold values from -0.25 to 0.25
- expand_weight: float32 [512, 2048], P('dp'), may hold values from -0.25 to 0.25
- reduce_weight: float32 [2048, 512], P('dp'), may hold values from -0.125 to 0.125
Outputs:
- layer_out: float32 [2, 4096, 512], P('dp', 'seq')
All inputs are finite; a program needn't handle non-finite values.
Results may differ from a plain program's by a relative error of at most 0.000069.
Values sent between devices are 32-bit elements; how exact they have to be, the bound alone decides.
A program may use at most 64 MiB of HBM per device.

v0:
```python
import jax
import jax.numpy as jnp
from jax import lax
from jax.sharding import PartitionSpec as P


def layer_norm(values, gain_row):
    average = jnp.mean(values, axis=-1, keepdims=True)
    centred = values - average
    variance = jnp.mean(centred * centred, axis=-1, keepdims=True)
    return centred * lax.rsqrt(variance + 1e-05) * gain_row


def make_fold(operand, block_rows):
    return jnp.dot(
        operand, block_rows, precision=lax.Precision.HIGHEST, preferred_element_type=jnp.float32
    )


def body(features, norm_gain, filters, level_weights, glu_weight, expand_weight, reduce_weight):
    batches, extent, channels = features.shape
    shallow = extent.bit_length() - 1
    deep_levels = lax.axis_size("seq").bit_length() - 1
    normed = layer_norm(features, norm_gain[0])
    group_count = lax.axis_size("seq")
    group_width = channels // group_count
    columns = lax.axis_index("seq") * group_width
    own_filters = lax.dynamic_slice_in_dim(filters, columns, group_width, 1)
    own_weights = lax.dynamic_slice_in_dim(level_weights, columns, group_width, 1)
    current = lax.all_to_all(normed, "seq", split_axis=2, concat_axis=1, tiled=True)
    whole_length = current.shape[1]
    all_levels = shallow + deep_levels
    channel_sum = jnp.zeros_like(current)
    for level_step in range(all_levels):
        spacing = 2**level_step
        earlier = jnp.concatenate(
            [
                jnp.zeros((batches, spacing, group_width), jnp.float32),
                current[:, : whole_length - spacing, :],
            ],
            axis=1,
        )
        channel_sum = channel_sum + own_weights[level_step] * (
            own_filters[2] * earlier + own_filters[3] * current
        )
        current = own_filters[0] * earlier + own_filters[1] * current
    channel_sum = channel_sum + own_weights[all_levels] * current
    detail_sum = lax.all_to_all(channel_sum, "seq", split_axis=1, concat_axis=2, tiled=True)
    row_count = batches * extent
    activated = jax.nn.gelu(detail_sum, approximate=False).reshape(row_count, channels)
    projected = make_fold(activated, lax.all_gather(glu_weight, "dp", axis=0, tiled=True))
    residual = features.reshape(row_count, channels) + projected[:, :channels] * jax.nn.sigmoid(
        projected[:, channels:]
    )
    second = layer_norm(residual, norm_gain[1])
    hidden = jax.nn.relu(make_fold(second, lax.all_gather(expand_weight, "dp", axis=0, tiled=True)))
    reduced = make_fold(hidden, lax.all_gather(reduce_weight, "dp", axis=0, tiled=True))
    return (residual + reduced).reshape(batches, extent, channels)


def solution(mesh):
    return jax.shard_map(
        body,
        mesh=mesh,
        in_specs=(P("dp", "seq", None), P(), P(), P(), P("dp", None), P("dp", None), P("dp", None)),
        out_specs=P("dp", "seq", None),
        check_vma=False,
    )
```

profile of v0, /device:TPU:0, one launch (start us, length us, event | category | flops | bytes accessed | tf_op | source)
XLA Modules:
  0.0 174.6 jit_solution(8305652701184986361)
XLA Ops:
  6.5 0.7 all-gather.4.cloned.1.call-update
  7.3 0.7 all-gather.6.cloned.1.call-update
  8.5 1.0 copy.31
  9.6 7.4 %all-to-all-start = ((f32[1,256,512]{1,0,2:T(1,128)}), f32[1,256,512]{1,0,2:T(1,128)S(1)}, u32[]{:S(2)}, u32[]{:S(2)}) async-start(f32[1,256,512]{1,0,2:T(1,128)} %copy.31), calls=%async_computation | async-start | bytes 1048576 | tf_op jit(solution)/shard_map/all_to_all | solution.py:30
  17.0 0.7 all-gather.8.cloned.1.call-update
  17.8 1.1 dynamic-slice_bitcast_fusion.12
  18.9 12.6 %all-to-all-done = f32[1,256,512]{1,0,2:T(1,128)S(1)} async-done(((f32[1,256,512]{1,0,2:T(1,128)}), f32[1,256,512]{1,0,2:T(1,128)S(1)}, u32[]{:S(2)}, u32[]{:S(2)}) %all-to-all-start) | async-done | bytes 524320 | tf_op jit(solution)/shard_map/all_to_all | solution.py:30
  31.5 0.2 multiply_add_fusion.8
  31.7 0.4 multiply_add_fusion.7
  32.1 0.2 multiply_add_fusion.6
  32.3 0.4 multiply_add_fusion.5
  32.7 0.2 multiply_add_fusion.4
  32.9 0.4 multiply_add_fusion.3
  33.3 0.2 multiply_add_fusion.2
  34.3 2.0 %fusion.6 = f32[1,4096,32]{1,2,0:T(8,128)S(1)} fusion(f32[1,3584,32]{1,2,0:T(8,128)S(1)} %slice.185, f32[1,3072,32]{1,2,0:T(8,128)S(1)} %slice.186, f32[1,2048,32]{1,2,0:T(8,128)S(1)} %slice.187, f32[1,4096,32]{1,2,0:T(8,128)S(1)} %multiply_add_fusion, f32[1,4096,32]{1,2,0:T(8,128)S(1)} %multiply_add_fusion.2, f32[1,4096,32]{1,2,0:T(8,128)S(1)} %multiply_add_fusion.3, ...), kind=kLoop, calls=%fused_computation.15 | loop fusion | flops 10747904 | bytes 9439488 | tf_op jit(solution)/shard_map/add | solution.py:47
  36.3 2.5 %copy.33 = f32[1,4096,32]{2,0,1:T(1,128)S(1)} copy(f32[1,4096,32]{1,2,0:T(8,128)S(1)} %fusion.6) | data formatting | bytes 1048576 | tf_op jit(solution)/shard_map/add | solution.py:47
  38.8 0.5 broadcast.255
  39.3 19.3 %reduce.2 = f32[4096,32]{1,0:T(8,128)} reduce(f32[4096,1,32]{2,1,0:T(1,128)S(1)} %bitcast.92, f32[]{:T(128)} %broadcast.255), dimensions={1}, to_apply=%bitcast.63.reduce_sub_computation | reduce | bytes 1048580
  58.6 2.6 %reshape.250 = f32[16,1,8192]{2,1,0:T(1,128)S(1)} reshape(f32[4096,32]{1,0:T(8,128)} %reduce.2) | data formatting | bytes 1048576
  61.2 18.4 %all_to_all.27 = f32[16,1,8192]{2,1,0:T(1,128)S(1)} all-to-all(f32[16,1,8192]{2,1,0:T(1,128)S(1)} %reshape.250), channel_id=1, replica_groups=mesh['seq'=16,'dp'=2] {'seq'}, dimensions={0} | all-to-all | bytes 1048576 | tf_op jit(solution)/shard_map/all_to_all | solution.py:48
  79.6 1.9 %reduce.3 = f32[16,8192]{1,0:T(8,128)S(1)} reduce(f32[16,1,8192]{2,1,0:T(1,128)S(1)} %all_to_all.27, f32[]{:T(128)} %broadcast.255), dimensions={1}, to_apply=%all_to_all.24.reduce_sub_computation | reduce | bytes 1048580 | tf_op jit(solution)/shard_map/all_to_all | solution.py:48
  81.6 3.5 %reshape.251 = f32[4096,1,32]{2,1,0:T(1,128)S(1)} reshape(f32[16,8192]{1,0:T(8,128)S(1)} %reduce.3) | data formatting | bytes 1048576
  85.1 2.1 %copy.34 = f32[1,4096,32]{1,2,0:T(8,128)S(1)} copy(f32[1,4096,32]{2,0,1:T(1,128)S(1)} %bitcast.91) | data formatting | bytes 1048576 | tf_op jit(solution)/shard_map/all_to_all | solution.py:48
  87.5 0.3 copy.37
  88.2 0.3 copy.35
  88.7 4.5 %fusion.17 = f32[256,1024]{1,0:T(8,128)S(1)} fusion(f32[512,1024]{1,0:T(8,128)} %all-gather.4.cloned.1.call-done, f32[256,512]{1,0:T(8,128)S(1)} %copy.43, f32[256,512]{1,0:T(8,128)S(1)} %copy.38), kind=kOutput, calls=%fused_computation.26 | convolution fusion | flops 1618608128 | bytes 4194304 | tf_op jit(solution)/shard_map/dot_general | solution.py:15
  93.3 0.2 fusion.139
  93.5 0.2 multiply_reduce_fusion
  93.7 9.3 %all-gather.6.cloned.1.call-done = f32[512,2048]{1,0:T(8,128)} async-done(((f32[256,2048]{1,0:T(8,128)}), f32[512,2048]{1,0:T(8,128)}) %all-gather.6.cloned.1.call-update) | async-done | bytes 4194320 | tf_op jit(solution)/shard_map/all_gather | solution.py:56
  103.1 5.7 %convolution_maximum_fusion = f32[256,2048]{1,0:T(8,128)S(1)} fusion(f32[512,2048]{1,0:T(8,128)} %all-gather.6.cloned.1.call-done, f32[256,512]{1,0:T(8,128)S(1)} %get-tuple-element.6, f32[512]{0:T(512)S(1)} %bitcast.106, f32[256]{0:T(256)S(1)} %add_rsqrt_fusion, f32[256]{0:T(256)S(1)} %broadcast_multiply_fusion.1), kind=kOutput, calls=%fused_computation | convolution fusion | flops 3222142976 | bytes 6819840 | tf_op jit(solution)/shard_map/dot_general | solution.py:15
  108.8 52.6 %all-gather.8.cloned.1.call-done = f32[2048,512]{1,0:T(8,128)} async-done(((f32[1024,512]{1,0:T(8,128)}), f32[2048,512]{1,0:T(8,128)}) %all-gather.8.cloned.1.call-update) | async-done | bytes 4194320 | tf_op jit(solution)/shard_map/all_gather | solution.py:57
  161.4 6.7 %fusion = f32[1,256,512]{2,1,0:T(8,128)} fusion(f32[256,512]{1,0:T(8,128)S(1)} %get-tuple-element.6, f32[256,2048]{1,0:T(8,128)S(1)} %convolution_maximum_fusion, f32[2048,512]{1,0:T(8,128)} %all-gather.8.cloned.1.call-done), kind=kOutput, calls=%fused_computation.2 | convolution fusion | flops 3221356544 | bytes 7340032 | tf_op jit(solution)/shard_map/dot_general | solution.py:15
  (35 shorter events, 2.3 us)
Async XLA Ops:
  6.5 11.2 %copy-start = (f32[4,512]{1,0:T(4,128)S(1)}, f32[4,512]{1,0:T(4,128)}, u32[]{:S(2)}) copy-start(f32[4,512]{1,0:T(4,128)} %param.9) | copy-start | bytes 24580
  6.5 1.5 copy-start.1
  6.5 1.8 %copy-start.2 = (f32[2,512]{1,0:T(2,128)S(1)}, f32[2,512]{1,0:T(2,128)}, u32[]{:S(2)}) copy-start(f32[2,512]{1,0:T(2,128)} %param.8) | copy-start | bytes 12292
  6.5 82.2 %all-gather.4.cloned.1.call-start = ((), (), s32[]{:S(2)}) async-start(), calls=%async_computation.2 | async-start | bytes 3145728 | tf_op jit(solution)/shard_map/all_gather | solution.py:51
  7.3 95.8 %all-gather.6.cloned.1.call-start = ((), (), s32[]{:S(2)}) async-start(), calls=%async_computation.3 | async-start | bytes 6291456 | tf_op jit(solution)/shard_map/all_gather | solution.py:56
  9.6 21.9 %all-to-all-start = ((f32[1,256,512]{1,0,2:T(1,128)}), f32[1,256,512]{1,0,2:T(1,128)S(1)}, u32[]{:S(2)}, u32[]{:S(2)}) async-start(f32[1,256,512]{1,0,2:T(1,128)} %copy.31), calls=%async_computation | async-start | bytes 1048576 | tf_op jit(solution)/shard_map/all_to_all | solution.py:30
  17.0 144.4 %all-gather.8.cloned.1.call-start = ((), (), s32[]{:S(2)}) async-start(), calls=%async_computation.4 | async-start | bytes 6291456 | tf_op jit(solution)/shard_map/all_gather | solution.py:57
Sparse Core Ops, SparseCore 0:
  8.9 35.8 all-gather.3
  46.3 56.7 all-gather.5
  104.6 56.7 all-gather.7
where the time goes:
time: 175 us
  waiting for transfers between devices  76.6 us (44%)
  other arithmetic  26.8 us (15%)
  blocking collectives  18.4 us (11%)
  matrix products  17 us (10%)
  local copies, waits for them, and re-layouts  15 us (9%)
  between operations  13.4 us (8%)
  starting transfers between devices  7.47 us (4%)
    all_gather x1, waiting for transfers between devices, body(): lax.all_gather(reduce_weight, 'dp', axis=0, tiled=True)  52.6 us
    unnamed x1, other arithmetic  19.3 us
    all_to_all x1, blocking collectives, body(): lax.all_to_all(channel_sum, 'seq', split_axis=1, concat_axis=2, tiled=True)  18.4 us
    dot_general x3, matrix products, make_fold(): jnp.dot(operand, block_rows, precision=lax.Precision.HIGHEST, preferred_e...  17 us
    all_to_all x1, waiting for transfers between devices, body(): lax.all_to_all(normed, 'seq', split_axis=2, concat_axis=1, tiled=True)  12.6 us
    all_gather x1, waiting for transfers between devices, body(): lax.all_gather(expand_weight, 'dp', axis=0, tiled=True)  9.34 us
    all_to_all x1, starting transfers between devices, body(): lax.all_to_all(normed, 'seq', split_axis=2, concat_axis=1, tiled=True)  7.39 us
    unnamed x12, local copies, waits for them, and re-layouts  6.96 us
  transfers between devices with their start and end apart: 4, of which 3 were waited for; matrix products, arithmetic and copies ran while one was open for 30% of the time, Pallas kernels for 0%

commit v1 on v0

v1 whole, which is shorter than its diff:
```python
import functools

import jax
import jax.numpy as jnp
from jax import lax
from jax.experimental import pallas as pl
from jax.experimental.pallas import tpu as pltpu
from jax.sharding import PartitionSpec as P

MESH = pl.DeviceIdType.MESH
LANES = 128
CHUNKS = 2
TILE = 256


def split(v):
    hi = v.astype(jnp.bfloat16)
    return hi, (v - hi.astype(jnp.float32)).astype(jnp.bfloat16)


def dot3(a_hi, a_lo, b):
    b_hi, b_lo = split(b)
    f = functools.partial(jnp.dot, preferred_element_type=jnp.float32)
    return f(a_hi, b_hi) + (f(a_hi, b_lo) + f(a_lo, b_hi))


def norm_rows(v, gain_row):
    centred = v - jnp.mean(v, axis=-1, keepdims=True)
    variance = jnp.mean(centred * centred, axis=-1, keepdims=True)
    return centred * lax.rsqrt(variance + 1e-05) * gain_row


def kernel(
    n_seq, n_dp, rows, splits,
    x_ref, gain_ref, taps_ref, lw_ref, glu_ref, expand_ref, reduce_ref, out_ref,
    window, level, local, recv1, send2, deep, a_hi_ref, a_lo_ref,
    glu_full, expand_full, reduce_full,
    halo_s, halo_r, a1_s, a1_r, a2_s, a2_r, own_sem, w_s, w_r, w_own,
):
    extent, channels = x_ref.shape
    shallow = extent.bit_length() - 1
    deep_levels = n_seq.bit_length() - 1
    all_levels = shallow + deep_levels
    me = lax.axis_index("seq")
    my_dp = lax.axis_index("dp")
    sibling = me + 1 - 2 * lax.rem(me, 2)
    pair = me + 2 - 4 * lax.rem(me // 2, 2)
    g = lax.rem(me, 4)
    owner_width = channels // splits
    cw = owner_width // CHUNKS
    hw = channels // CHUNKS

    def seq_peer(o):
        return lax.rem(me + o, n_seq)

    def dp_peer(o):
        return lax.rem(my_dp + o, n_dp)

    barrier = pltpu.get_barrier_semaphore()

    @pl.loop(1, n_seq)
    def _(o):
        pl.semaphore_signal(barrier, inc=1, device_id={"seq": seq_peer(o)}, device_id_type=MESH)

    for o in range(1, n_dp):
        pl.semaphore_signal(barrier, inc=1, device_id={"dp": dp_peer(o)}, device_id_type=MESH)

    weights = ((glu_ref, glu_full), (expand_ref, expand_full), (reduce_ref, reduce_full))
    for w, (src, full) in enumerate(weights):
        height = src.shape[0]
        at = pl.multiple_of(my_dp * height, height)
        pltpu.make_async_copy(src, full.at[pl.ds(at, height)], w_own.at[w]).start()

    @pl.loop(0, extent // 64)
    def _(i):
        at = pl.ds(pl.multiple_of(i * 64, 64), 64)
        to = pl.ds(pl.multiple_of(extent + i * 64, 64), 64)
        window[to, :] = norm_rows(x_ref[at, :], gain_ref[0:1, :])

    @pl.when(me == 0)
    def _():
        window[0:extent, :] = jnp.zeros((extent, channels), jnp.float32)

    pl.semaphore_wait(barrier, n_seq - 1 + n_dp - 1)

    def halo(h):
        cols = slice(h * hw, (h + 1) * hw)
        return pltpu.make_async_remote_copy(
            src_ref=window.at[extent : 2 * extent, cols],
            dst_ref=window.at[0:extent, cols],
            send_sem=halo_s.at[h], recv_sem=halo_r.at[h],
            device_id={"seq": lax.rem(me + 1, n_seq)}, device_id_type=MESH,
        )

    @pl.when(me < n_seq - 1)
    def _():
        for h in range(CHUNKS):
            halo(h).start()

    def piece_rows(w, shard, k):
        height = weights[w][0].shape[0]
        part = height // 4
        return pl.ds(pl.multiple_of(shard * height + k * part, part), part)

    def over_dp(w, o):
        src, full = weights[w]
        part = src.shape[0] // 4
        return pltpu.make_async_remote_copy(
            src_ref=src.at[pl.ds(pl.multiple_of(g * part, part), part)],
            dst_ref=full.at[piece_rows(w, my_dp, g)],
            send_sem=w_s.at[w, o - 1, 0], recv_sem=w_r.at[w, o - 1, 0],
            device_id={"dp": dp_peer(o)}, device_id_type=MESH,
        )

    def forward(w, o, kind):
        full = weights[w][1]
        shard = lax.rem(my_dp + n_dp - o, n_dp)
        piece = lax.rem(g + 2, 4) if kind == 3 else g
        at = full.at[piece_rows(w, shard, piece)]
        return pltpu.make_async_remote_copy(
            src_ref=at, dst_ref=at,
            send_sem=w_s.at[w, o - 1, kind], recv_sem=w_r.at[w, o - 1, kind],
            device_id={"seq": pair if kind == 1 else sibling}, device_id_type=MESH,
        )

    offsets = range(1, n_dp)

    def stage1(w):
        for o in offsets:
            over_dp(w, o).wait_recv()
            forward(w, o, 1).start()
            forward(w, o, 2).start()

    def stage2(w):
        for o in offsets:
            forward(w, o, 1).wait_recv()
            forward(w, o, 3).start()

    def stage3(w):
        src, full = weights[w]
        for o in offsets:
            forward(w, o, 2).wait_recv()
            forward(w, o, 3).wait_recv()
        height = src.shape[0]
        at = pl.multiple_of(my_dp * height, height)
        pltpu.make_async_copy(src, full.at[pl.ds(at, height)], w_own.at[w]).wait()

    for w in range(3):
        for o in offsets:
            over_dp(w, o).start()

    def block_of(ref, owner, h):
        at = pl.multiple_of((owner // splits) * rows, rows)
        if splits == 1:
            return ref.at[pl.ds(at, rows), h * cw : (h + 1) * cw]
        lane = pl.multiple_of(lax.rem(owner, splits) * owner_width + h * cw, LANES)
        return ref.at[pl.ds(at, rows), pl.ds(lane, cw)]

    def out1(h, dest):
        return pltpu.make_async_remote_copy(
            src_ref=block_of(level, dest, h), dst_ref=recv1.at[h, me],
            send_sem=a1_s.at[h, dest], recv_sem=a1_r.at[h, me],
            device_id={"seq": dest}, device_id_type=MESH,
        )

    def in1(h, source):
        return pltpu.make_async_remote_copy(
            src_ref=block_of(level, source, h), dst_ref=recv1.at[h, source],
            send_sem=a1_s.at[h, source], recv_sem=a1_r.at[h, source],
            device_id={"seq": source}, device_id_type=MESH,
        )

    def out2(h, dest):
        return pltpu.make_async_remote_copy(
            src_ref=send2.at[h, dest], dst_ref=block_of(deep, me, h),
            send_sem=a2_s.at[h, dest], recv_sem=a2_r.at[h, me],
            device_id={"seq": dest}, device_id_type=MESH,
        )

    def in2(h, source):
        return pltpu.make_async_remote_copy(
            src_ref=send2.at[h, source], dst_ref=block_of(deep, source, h),
            send_sem=a2_s.at[h, source], recv_sem=a2_r.at[h, source],
            device_id={"seq": source}, device_id_type=MESH,
        )

    for h in range(CHUNKS):

        @pl.when(me > 0)
        def _():
            halo(h).wait_recv()

        @pl.loop(0, hw // LANES)
        def _(c):
            lanes = pl.ds(pl.multiple_of(h * hw + c * LANES, LANES), LANES)
            tap = [taps_ref[i : i + 1, lanes] for i in range(4)]
            current = window[:, lanes]
            total = jnp.zeros((extent, LANES), jnp.float32)
            for step in range(shallow):
                earlier = pltpu.roll(current, 2**step, 0)
                weight = lw_ref[step : step + 1, lanes]
                total = total + (
                    (weight * tap[2]) * earlier[extent:] + (weight * tap[3]) * current[extent:]
                )
                current = tap[0] * earlier + tap[1] * current
            level[:, lanes] = current[extent:]
            local[:, lanes] = total

        own = pltpu.make_async_copy(block_of(level, me, h), recv1.at[h, me], own_sem.at[h])
        own.start()

        @pl.loop(1, n_seq)
        def _(o):
            out1(h, seq_peer(o)).start()

        own.wait()

    stage1(0)

    for h in range(CHUNKS):

        @pl.loop(1, n_seq)
        def _(o):
            in1(h, seq_peer(o)).wait_recv()

        @pl.loop(0, cw // LANES)
        def _(c):
            lanes = pl.ds(pl.multiple_of(c * LANES, LANES), LANES)
            first = h * cw + c * LANES
            if splits > 1:
                first = lax.rem(me, splits) * owner_width + first
            at = pl.ds(pl.multiple_of(first, LANES), LANES)
            tap = [taps_ref[i : i + 1, at][None] for i in range(4)]
            current = recv1[h, :, :, lanes]
            total = jnp.zeros_like(current)
            for step in range(deep_levels):
                shift = 2**step
                earlier = jnp.concatenate(
                    [jnp.zeros((shift, rows, LANES), jnp.float32), current[: n_seq - shift]], axis=0
                )
                weight = lw_ref[shallow + step : shallow + step + 1, at][None]
                total = total + (weight * tap[2]) * earlier + (weight * tap[3]) * current
                current = tap[0] * earlier + tap[1] * current
            total = total + lw_ref[all_levels : all_levels + 1, at][None] * current
            send2[h, :, :, lanes] = total

        own = pltpu.make_async_copy(send2.at[h, me], block_of(deep, me, h), own_sem.at[h])
        own.start()

        @pl.loop(1, n_seq)
        def _(o):
            out2(h, seq_peer(o)).start()

        own.wait()

    stage2(0)
    stage1(1)
    stage2(1)
    stage1(2)

    for h in range(CHUNKS):

        @pl.loop(1, n_seq)
        def _(o):
            in2(h, seq_peer(o)).wait_recv()

    @pl.loop(0, extent // 64)
    def _(i):
        at = pl.ds(pl.multiple_of(i * 64, 64), 64)
        v = local[at, :] + deep[at, :]
        hi, lo = split(0.5 * v * (1.0 + lax.erf(v * 0.7071067811865476)))
        a_hi_ref[at, :] = hi
        a_lo_ref[at, :] = lo

    stage3(0)

    @pl.loop(0, channels // TILE)
    def _(t):
        at = pl.ds(pl.multiple_of(t * TILE, TILE), TILE)
        gate_at = pl.ds(pl.multiple_of(channels + t * TILE, TILE), TILE)
        value = dot3(a_hi_ref[...], a_lo_ref[...], glu_full[:, at])
        gate = dot3(a_hi_ref[...], a_lo_ref[...], glu_full[:, gate_at])
        out_ref[:, at] = x_ref[:, at] + value * jax.nn.sigmoid(gate)

    stage2(2)

    @pl.loop(0, extent // 64)
    def _(i):
        at = pl.ds(pl.multiple_of(i * 64, 64), 64)
        hi, lo = split(norm_rows(out_ref[at, :], gain_ref[1:2, :]))
        a_hi_ref[at, :] = hi
        a_lo_ref[at, :] = lo

    stage3(1)
    stage3(2)

    @pl.loop(0, expand_full.shape[1] // TILE)
    def _(t):
        at = pl.ds(pl.multiple_of(t * TILE, TILE), TILE)
        hidden = jnp.maximum(dot3(a_hi_ref[...], a_lo_ref[...], expand_full[:, at]), 0.0)
        hi, lo = split(hidden)
        out_ref[...] += dot3(hi, lo, reduce_full[at, :])

    @pl.when(me < n_seq - 1)
    def _():
        for h in range(CHUNKS):
            halo(h).wait_send()

    for h in range(CHUNKS):

        @pl.loop(1, n_seq)
        def _(o):
            out1(h, seq_peer(o)).wait_send()
            out2(h, seq_peer(o)).wait_send()

    for w in range(3):
        for o in offsets:
            over_dp(w, o).wait_send()
            for kind in (1, 2, 3):
                forward(w, o, kind).wait_send()


def body(n_seq, n_dp, features, norm_gain, filters, level_weights, glu, expand, reduce):
    batches, extent, channels = features.shape
    rows = max(8, extent // n_seq)
    splits = n_seq * rows // extent
    cw = channels // splits // CHUNKS
    f32 = jnp.float32
    vmem = pl.BlockSpec(memory_space=pltpu.VMEM)
    hbm = pl.BlockSpec(memory_space=pl.ANY)
    dma = pltpu.SemaphoreType.DMA
    ff = expand.shape[1]
    out = pl.pallas_call(
        functools.partial(kernel, n_seq, n_dp, rows, splits),
        out_shape=jax.ShapeDtypeStruct((extent, channels), f32),
        in_specs=[vmem] * 4 + [hbm] * 3,
        out_specs=vmem,
        scratch_shapes=[
            pltpu.VMEM((2 * extent, channels), f32),
            pltpu.VMEM((extent, channels), f32),
            pltpu.VMEM((extent, channels), f32),
            pltpu.VMEM((CHUNKS, n_seq, rows, cw), f32),
            pltpu.VMEM((CHUNKS, n_seq, rows, cw), f32),
            pltpu.VMEM((extent, channels), f32),
            pltpu.VMEM((extent, channels), jnp.bfloat16),
            pltpu.VMEM((extent, channels), jnp.bfloat16),
            pltpu.VMEM((glu.shape[0] * n_dp, glu.shape[1]), f32),
            pltpu.VMEM((expand.shape[0] * n_dp, ff), f32),
            pltpu.VMEM((reduce.shape[0] * n_dp, channels), f32),
            dma((CHUNKS,)), dma((CHUNKS,)),
            dma((CHUNKS, n_seq)), dma((CHUNKS, n_seq)),
            dma((CHUNKS, n_seq)), dma((CHUNKS, n_seq)),
            dma((CHUNKS,)),
            dma((3, n_dp - 1, 4)), dma((3, n_dp - 1, 4)),
            dma((3,)),
        ],
        compiler_params=pltpu.CompilerParams(
            collective_id=0, has_side_effects=True, vmem_limit_bytes=44 * 1024 * 1024
        ),
        cost_estimate=pl.CostEstimate(
            flops=6 * extent * channels * (2 * channels + 2 * ff),
            bytes_accessed=4 * (3 * extent * channels), transcendentals=extent * channels * 2,
        ),
    )(features.reshape(extent, channels), norm_gain, filters, level_weights, glu, expand, reduce)
    return out.reshape(batches, extent, channels)


def solution(mesh):
    return jax.shard_map(
        functools.partial(body, mesh.shape["seq"], mesh.shape["dp"]),
        mesh=mesh,
        in_specs=(P("dp", "seq", None), P(), P(), P(), P("dp", None), P("dp", None), P("dp", None)),
        out_specs=P("dp", "seq", None),
        check_vma=False,
    )
```

time: 175 us -> 74.8 us (0.43)
  waiting for transfers between devices: 76.6 us -> 0 us
  Pallas kernels: 0 us -> 65.3 us
  other arithmetic: 26.8 us -> 0 us
  blocking collectives: 18.4 us -> 0 us
  matrix products: 17 us -> 0 us
  between operations: 13.4 us -> 0.02 us
  starting transfers between devices: 7.47 us -> 0 us
  local copies, waits for them, and re-layouts: 15 us -> 8.38 us
    pallas_call x0 -> x1, Pallas kernels: none -> 65.3 us  [body(): pl.pallas_call(functools.partial(kernel, n_seq, n_dp, rows, splits), out_...]
    all_gather x3 -> x0, waiting for transfers between devices: 62 us -> none  [the longest x1 52.6 us: body(): lax.all_gather(reduce_weight, 'dp', axis=0, tiled=True)]
    unnamed x1 -> x0, other arithmetic: 19.3 us -> none
    all_to_all x1 -> x0, blocking collectives: 18.4 us -> none  [body(): lax.all_to_all(channel_sum, 'seq', split_axis=1, concat_axis=2, tiled=True)]
    dot_general x3 -> x0, matrix products: 17 us -> none  [make_fold(): jnp.dot(operand, block_rows, precision=lax.Precision.HIGHEST, preferred_e...]
    all_to_all x1 -> x0, waiting for transfers between devices: 12.6 us -> none  [body(): lax.all_to_all(normed, 'seq', split_axis=2, concat_axis=1, tiled=True)]
    all_to_all x1 -> x0, starting transfers between devices: 7.39 us -> none  [body(): lax.all_to_all(normed, 'seq', split_axis=2, concat_axis=1, tiled=True)]
    add x12 -> x0, other arithmetic: 4.51 us -> none  [the longest x11 2.51 us: body(): current = own_filters[0] * earlier + own_filters[1] * current]
  transfers between devices with their start and end apart: 4 -> 0, of which waited for: 3 -> 0; matrix products, arithmetic and copies ran while one was open for 30% -> 0% of each run, Pallas kernels for 0% -> 0%
where the time goes in v1:
time: 74.8 us; the launch traced here: 73.7 us
  Pallas kernels  65.3 us (87%)
  local copies, waits for them, and re-layouts  8.38 us (11%)
    pallas_call x1, Pallas kernels, body(): pl.pallas_call(functools.partial(kernel, n_seq, n_dp, rows, splits), out_...  65.3 us
    unnamed x15, local copies, waits for them, and re-layouts  8.38 us

profile of v1, /device:TPU:0, one launch (start us, length us, event | category | flops | bytes accessed | tf_op | source)
XLA Modules:
  0.0 73.7 jit_solution(2473598496834306199)
XLA Ops:
  0.0 0.0 copy-start
  0.0 1.6 %copy-done = f32[256,2048]{1,0:T(8,128)S(1)} copy-done((f32[256,2048]{1,0:T(8,128)S(1)}, f32[256,2048]{1,0:T(8,128)}, u32[]{:S(2)}) %copy-start) | copy-done | bytes 2097176
  1.6 0.0 copy-start.1
  1.6 1.6 %copy-done.1 = f32[1024,512]{1,0:T(8,128)S(1)} copy-done((f32[1024,512]{1,0:T(8,128)S(1)}, f32[1024,512]{1,0:T(8,128)}, u32[]{:S(2)}) %copy-start.1) | copy-done | bytes 2097176
  3.2 0.0 copy-start.2
  3.2 1.2 %copy-done.2 = f32[256,1024]{1,0:T(8,128)S(1)} copy-done((f32[256,1024]{1,0:T(8,128)S(1)}, f32[256,1024]{1,0:T(8,128)}, u32[]{:S(2)}) %copy-start.2) | copy-done | bytes 1048600
  4.4 0.0 copy-start.3
  4.4 1.0 %copy-done.3 = f32[1,256,512]{2,1,0:T(8,128)S(1)} copy-done((f32[1,256,512]{2,1,0:T(8,128)S(1)}, f32[1,256,512]{2,1,0:T(8,128)}, u32[]{:S(2)}) %copy-start.3) | copy-done | bytes 524312
  5.5 0.0 copy-start.4
  5.5 0.8 %copy-done.4 = f32[13,512]{1,0:T(8,128)S(1)} copy-done((f32[13,512]{1,0:T(8,128)S(1)}, f32[13,512]{1,0:T(8,128)}, u32[]{:S(2)}) %copy-start.4) | copy-done | bytes 26648
  6.2 0.0 copy-start.5
  6.2 0.7 copy-done.5
  6.9 0.0 copy-start.6
  6.9 0.7 copy-done.6
  7.6 65.3 %shard_map.73 = f32[256,512]{1,0:T(8,128)S(1)} custom-call(f32[256,512]{1,0:T(8,128)S(1)} %bitcast.3, f32[2,512]{1,0:T(2,128)S(1)} %copy-done.6, f32[4,512]{1,0:T(4,128)S(1)} %copy-done.5, f32[13,512]{1,0:T(8,128)S(1)} %copy-done.4, f32[256,1024]{1,0:T(8,128)S(1)} %copy-done.2, f32[256,2048]{1,0:T(8,128)S(1)} %copy-done, f32[1024,512]{1,0:T(8,128)S(1)} %copy-done.1), custom_call_target="tpu_custom_call" | custom-call | flops 4026531840 | bytes 1572864 | tf_op jit(solution)/shard_map/pallas_call | solution.py:333
  72.9 0.8 %copy.9 = f32[1,256,512]{2,1,0:T(8,128)} copy(f32[1,256,512]{2,1,0:T(8,128)S(1)} %bitcast.2) | data formatting | bytes 1048576
Async XLA Ops:
  0.0 1.6 %copy-start = (f32[256,2048]{1,0:T(8,128)S(1)}, f32[256,2048]{1,0:T(8,128)}, u32[]{:S(2)}) copy-start(f32[256,2048]{1,0:T(8,128)} %expand_ref.1) | copy-start | bytes 6291460
  1.6 1.6 %copy-start.1 = (f32[1024,512]{1,0:T(8,128)S(1)}, f32[1024,512]{1,0:T(8,128)}, u32[]{:S(2)}) copy-start(f32[1024,512]{1,0:T(8,128)} %reduce_ref.1) | copy-start | bytes 6291460
  3.2 1.2 %copy-start.2 = (f32[256,1024]{1,0:T(8,128)S(1)}, f32[256,1024]{1,0:T(8,128)}, u32[]{:S(2)}) copy-start(f32[256,1024]{1,0:T(8,128)} %glu_ref.1) | copy-start | bytes 3145732
  4.4 1.0 %copy-start.3 = (f32[1,256,512]{2,1,0:T(8,128)S(1)}, f32[1,256,512]{2,1,0:T(8,128)}, u32[]{:S(2)}) copy-start(f32[1,256,512]{2,1,0:T(8,128)} %param.7) | copy-start | bytes 1572868
  5.5 0.8 %copy-start.4 = (f32[13,512]{1,0:T(8,128)S(1)}, f32[13,512]{1,0:T(8,128)}, u32[]{:S(2)}) copy-start(f32[13,512]{1,0:T(8,128)} %lw_ref.1) | copy-start | bytes 79876
  6.2 0.7 copy-start.5
  6.9 0.7 copy-start.6

commit v2 on v1

--- a/solution.py
+++ b/solution.py
@@ -32,10 +32,10 @@
 
 def kernel(
     n_seq, n_dp, rows, splits,
-    x_ref, gain_ref, taps_ref, lw_ref, glu_ref, expand_ref, reduce_ref, out_ref,
-    window, level, local, recv1, send2, deep, a_hi_ref, a_lo_ref,
+    x_in, gain_in, taps_in, lw_in, glu_ref, expand_ref, reduce_ref, out_ref,
+    x_ref, gain_ref, taps_ref, lw_ref, window, level, local, recv1, send2, deep, a_hi_ref, a_lo_ref,
     glu_full, expand_full, reduce_full,
-    halo_s, halo_r, a1_s, a1_r, a2_s, a2_r, own_sem, w_s, w_r, w_own,
+    halo_s, halo_r, a1_s, a1_r, a2_s, a2_r, own_sem, w_s, w_r, w_own, in_sem,
 ):
     extent, channels = x_ref.shape
     shallow = extent.bit_length() - 1
@@ -46,15 +46,19 @@
     sibling = me + 1 - 2 * lax.rem(me, 2)
     pair = me + 2 - 4 * lax.rem(me // 2, 2)
     g = lax.rem(me, 4)
-    owner_width = channels // splits
-    cw = owner_width // CHUNKS
     hw = channels // CHUNKS
+    cw = hw // splits
 
     def seq_peer(o):
         return lax.rem(me + o, n_seq)
 
     def dp_peer(o):
         return lax.rem(my_dp + o, n_dp)
+
+    inputs = ((x_in, x_ref), (gain_in, gain_ref), (taps_in, taps_ref), (lw_in, lw_ref))
+    copies = [pltpu.make_async_copy(a, b, in_sem.at[i]) for i, (a, b) in enumerate(inputs)]
+    for copy in copies:
+        copy.start()
 
     barrier = pltpu.get_barrier_semaphore()
 
@@ -65,11 +69,16 @@
     for o in range(1, n_dp):
         pl.semaphore_signal(barrier, inc=1, device_id={"dp": dp_peer(o)}, device_id_type=MESH)
 
-    weights = ((glu_ref, glu_full), (expand_ref, expand_full), (reduce_ref, reduce_full))
-    for w, (src, full) in enumerate(weights):
+    weights = ((glu_ref, glu_full, 4), (expand_ref, expand_full, 4), (reduce_ref, reduce_full, 2))
+
+    def own_shard(w):
+        src, full, _ = weights[w]
         height = src.shape[0]
         at = pl.multiple_of(my_dp * height, height)
-        pltpu.make_async_copy(src, full.at[pl.ds(at, height)], w_own.at[w]).start()
+        return pltpu.make_async_copy(src, full.at[pl.ds(at, height)], w_own.at[w])
+
+    for copy in copies:
+        copy.wait()
 
     @pl.loop(0, extent // 64)
     def _(i):
@@ -99,15 +108,16 @@
 
     def piece_rows(w, shard, k):
         height = weights[w][0].shape[0]
-        part = height // 4
+        part = height // weights[w][2]
         return pl.ds(pl.multiple_of(shard * height + k * part, part), part)
 
     def over_dp(w, o):
-        src, full = weights[w]
-        part = src.shape[0] // 4
-        return pltpu.make_async_remote_copy(
-            src_ref=src.at[pl.ds(pl.multiple_of(g * part, part), part)],
-            dst_ref=full.at[piece_rows(w, my_dp, g)],
+        src, full, pieces = weights[w]
+        part = src.shape[0] // pieces
+        mine = lax.rem(g, pieces)
+        return pltpu.make_async_remote_copy(
+            src_ref=src.at[pl.ds(pl.multiple_of(mine * part, part), part)],
+            dst_ref=full.at[piece_rows(w, my_dp, mine)],
             send_sem=w_s.at[w, o - 1, 0], recv_sem=w_r.at[w, o - 1, 0],
             device_id={"dp": dp_peer(o)}, device_id_type=MESH,
         )
@@ -115,7 +125,7 @@
     def forward(w, o, kind):
         full = weights[w][1]
         shard = lax.rem(my_dp + n_dp - o, n_dp)
-        piece = lax.rem(g + 2, 4) if kind == 3 else g
+        piece = lax.rem(g + 2, 4) if kind == 3 else lax.rem(g, weights[w][2])
         at = full.at[piece_rows(w, shard, piece)]
         return pltpu.make_async_remote_copy(
             src_ref=at, dst_ref=at,
@@ -128,7 +138,8 @@
     def stage1(w):
         for o in offsets:
             over_dp(w, o).wait_recv()
-            forward(w, o, 1).start()
+            if weights[w][2] == 4:
+                forward(w, o, 1).start()
             forward(w, o, 2).start()
 
     def stage2(w):
@@ -137,23 +148,25 @@
             forward(w, o, 3).start()
 
     def stage3(w):
-        src, full = weights[w]
         for o in offsets:
             forward(w, o, 2).wait_recv()
-            forward(w, o, 3).wait_recv()
-        height = src.shape[0]
-        at = pl.multiple_of(my_dp * height, height)
-        pltpu.make_async_copy(src, full.at[pl.ds(at, height)], w_own.at[w]).wait()
-
-    for w in range(3):
+            if weights[w][2] == 4:
+                forward(w, o, 3).wait_recv()
+
+    def send_over_dp(w):
         for o in offsets:
             over_dp(w, o).start()
+
+    send_over_dp(0)
+    send_over_dp(1)
+    for w in range(3):
+        own_shard(w).start()
 
     def block_of(ref, owner, h):
         at = pl.multiple_of((owner // splits) * rows, rows)
         if splits == 1:
             return ref.at[pl.ds(at, rows), h * cw : (h + 1) * cw]
-        lane = pl.multiple_of(lax.rem(owner, splits) * owner_width + h * cw, LANES)
+        lane = pl.multiple_of(h * hw + lax.rem(owner, splits) * cw, LANES)
         return ref.at[pl.ds(at, rows), pl.ds(lane, cw)]
 
     def out1(h, dest):
@@ -216,6 +229,7 @@
         own.wait()
 
     stage1(0)
+    send_over_dp(2)
 
     for h in range(CHUNKS):
 
@@ -226,9 +240,9 @@
         @pl.loop(0, cw // LANES)
         def _(c):
             lanes = pl.ds(pl.multiple_of(c * LANES, LANES), LANES)
-            first = h * cw + c * LANES
+            first = h * hw + c * LANES
             if splits > 1:
-                first = lax.rem(me, splits) * owner_width + first
+                first = first + lax.rem(me, splits) * cw
             at = pl.ds(pl.multiple_of(first, LANES), LANES)
             tap = [taps_ref[i : i + 1, at][None] for i in range(4)]
             current = recv1[h, :, :, lanes]
@@ -252,11 +266,11 @@
             out2(h, seq_peer(o)).start()
 
         own.wait()
-
-    stage2(0)
-    stage1(1)
+        if h == 0:
+            stage2(0)
+            stage1(1)
+
     stage2(1)
-    stage1(2)
 
     for h in range(CHUNKS):
 
@@ -272,6 +286,7 @@
         a_hi_ref[at, :] = hi
         a_lo_ref[at, :] = lo
 
+    own_shard(0).wait()
     stage3(0)
 
     @pl.loop(0, channels // TILE)
@@ -282,7 +297,7 @@
         gate = dot3(a_hi_ref[...], a_lo_ref[...], glu_full[:, gate_at])
         out_ref[:, at] = x_ref[:, at] + value * jax.nn.sigmoid(gate)
 
-    stage2(2)
+    stage1(2)
 
     @pl.loop(0, extent // 64)
     def _(i):
@@ -291,15 +306,24 @@
         a_hi_ref[at, :] = hi
         a_lo_ref[at, :] = lo
 
+    own_shard(1).wait()
+    own_shard(2).wait()
     stage3(1)
+
+    def feed_forward(shard):
+        height = reduce_ref.shape[0]
+
+        @pl.loop(0, height // TILE)
+        def _(t):
+            at = pl.ds(pl.multiple_of(shard * height + t * TILE, TILE), TILE)
+            hidden = jnp.maximum(dot3(a_hi_ref[...], a_lo_ref[...], expand_full[:, at]), 0.0)
+            hi, lo = split(hidden)
+            out_ref[...] += dot3(hi, lo, reduce_full[at, :])
+
+    feed_forward(my_dp)
     stage3(2)
-
-    @pl.loop(0, expand_full.shape[1] // TILE)
-    def _(t):
-        at = pl.ds(pl.multiple_of(t * TILE, TILE), TILE)
-        hidden = jnp.maximum(dot3(a_hi_ref[...], a_lo_ref[...], expand_full[:, at]), 0.0)
-        hi, lo = split(hidden)
-        out_ref[...] += dot3(hi, lo, reduce_full[at, :])
+    for o in offsets:
+        feed_forward(dp_peer(o))
 
     @pl.when(me < n_seq - 1)
     def _():
@@ -316,7 +340,7 @@
     for w in range(3):
         for o in offsets:
             over_dp(w, o).wait_send()
-            for kind in (1, 2, 3):
+            for kind in (1, 2, 3) if weights[w][2] == 4 else (2,):
                 forward(w, o, kind).wait_send()
 
 
@@ -333,9 +357,13 @@
     out = pl.pallas_call(
         functools.partial(kernel, n_seq, n_dp, rows, splits),
         out_shape=jax.ShapeDtypeStruct((extent, channels), f32),
-        in_specs=[vmem] * 4 + [hbm] * 3,
+        in_specs=[hbm] * 7,
         out_specs=vmem,
         scratch_shapes=[
+            pltpu.VMEM((extent, channels), f32),
+            pltpu.VMEM(norm_gain.shape, f32),
+            pltpu.VMEM(filters.shape, f32),
+            pltpu.VMEM(level_weights.shape, f32),
             pltpu.VMEM((2 * extent, channels), f32),
             pltpu.VMEM((extent, channels), f32),
             pltpu.VMEM((extent, channels), f32),
@@ -352,10 +380,10 @@
             dma((CHUNKS, n_seq)), dma((CHUNKS, n_seq)),
             dma((CHUNKS,)),
             dma((3, n_dp - 1, 4)), dma((3, n_dp - 1, 4)),
-            dma((3,)),
+            dma((3,)), dma((4,)),
         ],
         compiler_params=pltpu.CompilerParams(
-            collective_id=0, has_side_effects=True, vmem_limit_bytes=44 * 1024 * 1024
+            collective_id=0, has_side_effects=True, vmem_limit_bytes=60 * 1024 * 1024
         ),
         cost_estimate=pl.CostEstimate(
             flops=6 * extent * channels * (2 * channels + 2 * ff),

time: 74.8 us -> 61.8 us (0.83); the launches traced: 73.7 us -> 61.6 us
  local copies, waits for them, and re-layouts: 8.38 us -> 1.87 us
  Pallas kernels: 65.3 us -> 59.8 us
    unnamed x15 -> x1, local copies, waits for them, and re-layouts: 8.38 us -> 1.87 us
    pallas_call x1, Pallas kernels: 65.3 us -> 59.8 us  [body(): pl.pallas_call(functools.partial(kernel, n_seq, n_dp, rows, splits), out_...]
where the time goes in v2:
time: 61.8 us; the launch traced here: 61.6 us
  Pallas kernels  59.8 us (97%)
  local copies, waits for them, and re-layouts  1.87 us (3%)
    pallas_call x1, Pallas kernels, body(): pl.pallas_call(functools.partial(kernel, n_seq, n_dp, rows, splits), out_...  59.8 us
    unnamed x1, local copies, waits for them, and re-layouts  1.87 us

profile of v2, /device:TPU:0, one launch (start us, length us, event | category | flops | bytes accessed | tf_op | source)
XLA Modules:
  0.0 61.6 jit_solution(4360842546600091478)
XLA Ops:
  0.0 59.8 %shard_map.73 = f32[256,512]{1,0:T(8,128)} custom-call(f32[256,512]{1,0:T(8,128)} %bitcast.3, f32[2,512]{1,0:T(2,128)} %gain_in.1, f32[4,512]{1,0:T(4,128)} %taps_in.1, f32[13,512]{1,0:T(8,128)} %lw_in.1, f32[256,1024]{1,0:T(8,128)} %glu_ref.1, f32[256,2048]{1,0:T(8,128)} %expand_ref.1, f32[1024,512]{1,0:T(8,128)} %reduce_ref.1), custom_call_target="tpu_custom_call" | custom-call | flops 4026531840 | bytes 1572864 | tf_op jit(solution)/shard_map/pallas_call | solution.py:357
  59.8 1.9 %copy.9 = f32[1,256,512]{2,1,0:T(8,128)} copy(f32[1,256,512]{2,1,0:T(8,128)} %bitcast.2) | data formatting | bytes 1048576

commit v3 on v2

--- a/solution.py
+++ b/solution.py
@@ -34,7 +34,7 @@
     n_seq, n_dp, rows, splits,
     x_in, gain_in, taps_in, lw_in, glu_ref, expand_ref, reduce_ref, out_ref,
     x_ref, gain_ref, taps_ref, lw_ref, window, level, local, recv1, send2, deep, a_hi_ref, a_lo_ref,
-    glu_full, expand_full, reduce_full,
+    glu_full, expand_full, reduce_full, proj,
     halo_s, halo_r, a1_s, a1_r, a2_s, a2_r, own_sem, w_s, w_r, w_own, in_sem,
 ):
     extent, channels = x_ref.shape
@@ -270,32 +270,41 @@
             stage2(0)
             stage1(1)
 
-    stage2(1)
-
+    own_shard(0).wait()
     for h in range(CHUNKS):
+        cols = slice(h * hw, (h + 1) * hw)
 
         @pl.loop(1, n_seq)
         def _(o):
             in2(h, seq_peer(o)).wait_recv()
 
-    @pl.loop(0, extent // 64)
-    def _(i):
-        at = pl.ds(pl.multiple_of(i * 64, 64), 64)
-        v = local[at, :] + deep[at, :]
-        hi, lo = split(0.5 * v * (1.0 + lax.erf(v * 0.7071067811865476)))
-        a_hi_ref[at, :] = hi
-        a_lo_ref[at, :] = lo
-
-    own_shard(0).wait()
-    stage3(0)
-
-    @pl.loop(0, channels // TILE)
-    def _(t):
-        at = pl.ds(pl.multiple_of(t * TILE, TILE), TILE)
-        gate_at = pl.ds(pl.multiple_of(channels + t * TILE, TILE), TILE)
-        value = dot3(a_hi_ref[...], a_lo_ref[...], glu_full[:, at])
-        gate = dot3(a_hi_ref[...], a_lo_ref[...], glu_full[:, gate_at])
-        out_ref[:, at] = x_ref[:, at] + value * jax.nn.sigmoid(gate)
+        @pl.loop(0, extent // 64)
+        def _(i):
+            at = pl.ds(pl.multiple_of(i * 64, 64), 64)
+            v = local[at, cols] + deep[at, cols]
+            hi, lo = split(0.5 * v * (1.0 + lax.erf(v * 0.7071067811865476)))
+            a_hi_ref[at, cols] = hi
+            a_lo_ref[at, cols] = lo
+
+        if h == 0:
+            stage3(0)
+        if h == CHUNKS - 1:
+            stage2(1)
+
+        @pl.loop(0, channels // TILE)
+        def _(t):
+            at = pl.ds(pl.multiple_of(t * TILE, TILE), TILE)
+            gate_at = pl.ds(pl.multiple_of(channels + t * TILE, TILE), TILE)
+            value = dot3(a_hi_ref[:, cols], a_lo_ref[:, cols], glu_full[cols, at])
+            gate = dot3(a_hi_ref[:, cols], a_lo_ref[:, cols], glu_full[cols, gate_at])
+            if h > 0:
+                value = value + proj[:, at]
+                gate = gate + proj[:, gate_at]
+            if h < CHUNKS - 1:
+                proj[:, at] = value
+                proj[:, gate_at] = gate
+            else:
+                out_ref[:, at] = x_ref[:, at] + value * jax.nn.sigmoid(gate)
 
     stage1(2)
 
@@ -313,7 +322,7 @@
     def feed_forward(shard):
         height = reduce_ref.shape[0]
 
-        @pl.loop(0, height // TILE)
+        @pl.loop(0, height // TILE, unroll=min(2, height // TILE))
         def _(t):
             at = pl.ds(pl.multiple_of(shard * height + t * TILE, TILE), TILE)
             hidden = jnp.maximum(dot3(a_hi_ref[...], a_lo_ref[...], expand_full[:, at]), 0.0)
@@ -375,6 +384,7 @@
             pltpu.VMEM((glu.shape[0] * n_dp, glu.shape[1]), f32),
             pltpu.VMEM((expand.shape[0] * n_dp, ff), f32),
             pltpu.VMEM((reduce.shape[0] * n_dp, channels), f32),
+            pltpu.VMEM((extent, 2 * channels), f32),
             dma((CHUNKS,)), dma((CHUNKS,)),
             dma((CHUNKS, n_seq)), dma((CHUNKS, n_seq)),
             dma((CHUNKS, n_seq)), dma((CHUNKS, n_seq)),

time: 61.8 us -> 59.5 us (0.963)
  Pallas kernels: 59.8 us -> 57.4 us
    pallas_call x1, Pallas kernels: 59.8 us -> 57.4 us  [body(): pl.pallas_call(functools.partial(kernel, n_seq, n_dp, rows, splits), out_...]
where the time goes in v3:
time: 59.5 us; the launch traced here: 59.3 us
  Pallas kernels  57.4 us (96%)
  local copies, waits for them, and re-layouts  1.87 us (3%)
    pallas_call x1, Pallas kernels, body(): pl.pallas_call(functools.partial(kernel, n_seq, n_dp, rows, splits), out_...  57.4 us
    unnamed x1, local copies, waits for them, and re-layouts  1.87 us

profile of v3, /device:TPU:0, one launch (start us, length us, event | category | flops | bytes accessed | tf_op | source)
XLA Modules:
  0.0 59.3 jit_solution(1252795415804404039)
XLA Ops:
  0.0 57.4 %shard_map.73 = f32[256,512]{1,0:T(8,128)} custom-call(f32[256,512]{1,0:T(8,128)} %bitcast.3, f32[2,512]{1,0:T(2,128)} %gain_in.1, f32[4,512]{1,0:T(4,128)} %taps_in.1, f32[13,512]{1,0:T(8,128)} %lw_in.1, f32[256,1024]{1,0:T(8,128)} %glu_ref.1, f32[256,2048]{1,0:T(8,128)} %expand_ref.1, f32[1024,512]{1,0:T(8,128)} %reduce_ref.1), custom_call_target="tpu_custom_call" | custom-call | flops 4026531840 | bytes 1572864 | tf_op jit(solution)/shard_map/pallas_call | solution.py:366
  57.4 1.9 %copy.9 = f32[1,256,512]{2,1,0:T(8,128)} copy(f32[1,256,512]{2,1,0:T(8,128)} %bitcast.2) | data formatting | bytes 1048576

commit v4 on v3

--- a/solution.py
+++ b/solution.py
@@ -9,7 +9,7 @@
 
 MESH = pl.DeviceIdType.MESH
 LANES = 128
-CHUNKS = 2
+GROUPS = 2
 TILE = 256
 
 
@@ -31,7 +31,7 @@
 
 
 def kernel(
-    n_seq, n_dp, rows, splits,
+    n_seq, n_dp, rows, splits, chunks,
     x_in, gain_in, taps_in, lw_in, glu_ref, expand_ref, reduce_ref, out_ref,
     x_ref, gain_ref, taps_ref, lw_ref, window, level, local, recv1, send2, deep, a_hi_ref, a_lo_ref,
     glu_full, expand_full, reduce_full, proj,
@@ -46,7 +46,7 @@
     sibling = me + 1 - 2 * lax.rem(me, 2)
     pair = me + 2 - 4 * lax.rem(me // 2, 2)
     g = lax.rem(me, 4)
-    hw = channels // CHUNKS
+    hw = channels // chunks
     cw = hw // splits
 
     def seq_peer(o):
@@ -103,7 +103,7 @@
 
     @pl.when(me < n_seq - 1)
     def _():
-        for h in range(CHUNKS):
+        for h in range(chunks):
             halo(h).start()
 
     def piece_rows(w, shard, k):
@@ -197,7 +197,7 @@
             device_id={"seq": source}, device_id_type=MESH,
         )
 
-    for h in range(CHUNKS):
+    for h in range(chunks):
 
         @pl.when(me > 0)
         def _():
@@ -231,7 +231,7 @@
     stage1(0)
     send_over_dp(2)
 
-    for h in range(CHUNKS):
+    for h in range(chunks):
 
         @pl.loop(1, n_seq)
         def _(o):
@@ -266,17 +266,21 @@
             out2(h, seq_peer(o)).start()
 
         own.wait()
-        if h == 0:
+        if h == chunks // 2 - 1:
             stage2(0)
             stage1(1)
 
     own_shard(0).wait()
-    for h in range(CHUNKS):
-        cols = slice(h * hw, (h + 1) * hw)
-
-        @pl.loop(1, n_seq)
-        def _(o):
-            in2(h, seq_peer(o)).wait_recv()
+    gw = channels // GROUPS
+    per_group = chunks // GROUPS
+    for h in range(GROUPS):
+        cols = slice(h * gw, (h + 1) * gw)
+
+        for k in range(h * per_group, (h + 1) * per_group):
+
+            @pl.loop(1, n_seq)
+            def _(o):
+                in2(k, seq_peer(o)).wait_recv()
 
         @pl.loop(0, extent // 64)
         def _(i):
@@ -288,7 +292,7 @@
 
         if h == 0:
             stage3(0)
-        if h == CHUNKS - 1:
+        if h == GROUPS - 1:
             stage2(1)
 
         @pl.loop(0, channels // TILE)
@@ -300,7 +304,7 @@
             if h > 0:
                 value = value + proj[:, at]
                 gate = gate + proj[:, gate_at]
-            if h < CHUNKS - 1:
+            if h < GROUPS - 1:
                 proj[:, at] = value
                 proj[:, gate_at] = gate
             else:
@@ -336,10 +340,10 @@
 
     @pl.when(me < n_seq - 1)
     def _():
-        for h in range(CHUNKS):
+        for h in range(chunks):
             halo(h).wait_send()
 
-    for h in range(CHUNKS):
+    for h in range(chunks):
 
         @pl.loop(1, n_seq)
         def _(o):
@@ -357,14 +361,15 @@
     batches, extent, channels = features.shape
     rows = max(8, extent // n_seq)
     splits = n_seq * rows // extent
-    cw = channels // splits // CHUNKS
+    chunks = max(GROUPS, channels // LANES // splits)
+    cw = channels // splits // chunks
     f32 = jnp.float32
     vmem = pl.BlockSpec(memory_space=pltpu.VMEM)
     hbm = pl.BlockSpec(memory_space=pl.ANY)
     dma = pltpu.SemaphoreType.DMA
     ff = expand.shape[1]
     out = pl.pallas_call(
-        functools.partial(kernel, n_seq, n_dp, rows, splits),
+        functools.partial(kernel, n_seq, n_dp, rows, splits, chunks),
         out_shape=jax.ShapeDtypeStruct((extent, channels), f32),
         in_specs=[hbm] * 7,
         out_specs=vmem,
@@ -376,8 +381,8 @@
             pltpu.VMEM((2 * extent, channels), f32),
             pltpu.VMEM((extent, channels), f32),
             pltpu.VMEM((extent, channels), f32),
-            pltpu.VMEM((CHUNKS, n_seq, rows, cw), f32),
-            pltpu.VMEM((CHUNKS, n_seq, rows, cw), f32),
+            pltpu.VMEM((chunks, n_seq, rows, cw), f32),
+            pltpu.VMEM((chunks, n_seq, rows, cw), f32),
             pltpu.VMEM((extent, channels), f32),
             pltpu.VMEM((extent, channels), jnp.bfloat16),
             pltpu.VMEM((extent, channels), jnp.bfloat16),
@@ -385,10 +390,10 @@
             pltpu.VMEM((expand.shape[0] * n_dp, ff), f32),
             pltpu.VMEM((reduce.shape[0] * n_dp, channels), f32),
             pltpu.VMEM((extent, 2 * channels), f32),
-            dma((CHUNKS,)), dma((CHUNKS,)),
-            dma((CHUNKS, n_seq)), dma((CHUNKS, n_seq)),
-            dma((CHUNKS, n_seq)), dma((CHUNKS, n_seq)),
-            dma((CHUNKS,)),
+            dma((chunks,)), dma((chunks,)),
+            dma((chunks, n_seq)), dma((chunks, n_seq)),
+            dma((chunks, n_seq)), dma((chunks, n_seq)),
+            dma((chunks,)),
             dma((3, n_dp - 1, 4)), dma((3, n_dp - 1, 4)),
             dma((3,)), dma((4,)),
         ],

time: 59.5 us -> 61 us (1.025)
  Pallas kernels: 57.4 us -> 59 us
    pallas_call x1, Pallas kernels: 57.4 us -> 59 us  [body(): pl.pallas_call(functools.partial(kernel, n_seq, n_dp, rows, splits, chunk...]
where the time goes in v4:
time: 61 us; the launch traced here: 60.9 us
  Pallas kernels  59 us (97%)
  local copies, waits for them, and re-layouts  1.87 us (3%)
    pallas_call x1, Pallas kernels, body(): pl.pallas_call(functools.partial(kernel, n_seq, n_dp, rows, splits, chunk...  59 us
    unnamed x1, local copies, waits for them, and re-layouts  1.87 us

profile of v4, /device:TPU:0, one launch (start us, length us, event | category | flops | bytes accessed | tf_op | source)
XLA Modules:
  0.0 60.9 jit_solution(10600547829404769685)
XLA Ops:
  0.0 59.0 %shard_map.73 = f32[256,512]{1,0:T(8,128)} custom-call(f32[256,512]{1,0:T(8,128)} %bitcast.3, f32[2,512]{1,0:T(2,128)} %gain_in.1, f32[4,512]{1,0:T(4,128)} %taps_in.1, f32[13,512]{1,0:T(8,128)} %lw_in.1, f32[256,1024]{1,0:T(8,128)} %glu_ref.1, f32[256,2048]{1,0:T(8,128)} %expand_ref.1, f32[1024,512]{1,0:T(8,128)} %reduce_ref.1), custom_call_target="tpu_custom_call" | custom-call | flops 4026531840 | bytes 1572864 | tf_op jit(solution)/shard_map/pallas_call | solution.py:371
  59.0 1.9 %copy.9 = f32[1,256,512]{2,1,0:T(8,128)} copy(f32[1,256,512]{2,1,0:T(8,128)} %bitcast.2) | data formatting | bytes 1048576
